TPU v7x, 32 devices: a whole 2x2x4 slice. The times are simulated.
32 devices in a mesh: groups: 2 (over y), patch: 4 (over z), tensor: 4 (over x, core).
Axes of the slice: x: 2, y: 2, z: 4, core: 2. Of those that a mesh axis runs over, the one named last changes fastest.
Arguments:
- hidden: bfloat16 [1152, 3072], P(('groups', 'patch'), 'tensor'), parts along dimension 0, may hold values from -40 to 40
- modulation: bfloat16 [3, 3072], P(None, 'tensor'), may hold values from -3 to 3
- w_qkv: bfloat16 [3072, 8, 384], P('patch', 'tensor'), may hold values from -0.109375 to 0.109375
- w_out: bfloat16 [3072, 1024], P('patch', 'tensor'), may hold values from -0.1875 to 0.1875
- qk_gain: float32 [2, 8, 128], P(None, 'tensor'), may hold values from 0.5 to 100
- stale: bfloat16 [2, 1152, 1024], P(None, 'groups', 'tensor'), parts along dimension 1, may hold values from -6 to 6
- offsets: int32 [8], P(('groups', 'patch')), parts along dimension 0, may hold values from 0 to 384, as said below
- text_count: int32 [2], P('groups'), parts along dimension 0, may hold values from 1 to 64
- exponents: int32 [2, 8, 8], P(None, ('groups', 'patch'), 'tensor'), parts along dimension 1, may hold values from -9 to -4
Outputs:
- result: bfloat16 [1152, 3072], P(('groups', 'patch'), 'tensor'), parts along dimension 0
There are 2 independent parts, one for each index of `groups`. A program takes and returns all parts, laid end to end along the dimension named above; an argument that names none is the same for every part. Nothing has to cross between parts.
Inputs may be any that keep to these rules, and one draw needn't show every extreme that they name: `offsets`: the image tokens of the patches start at distinct multiples of 128.
All inputs are finite; a program needn't handle non-finite values.
Results may differ from a plain program's by a relative error of at most 0.003.
The roundings to bfloat16 on the way count: a program that leaves them out, or rounds other values in their place, can miss the bound.
Values may be sent and summed in bfloat16 or wider, within the bound.
A program may use at most 128 MiB of HBM per device.

v0:
```python
import jax
import jax.numpy as jnp
from jax import lax
from jax.sharding import PartitionSpec as P

TXT_DEV = 16


def rotate(values, cosine, sine):
    half = values.shape[-1] // 2
    turned = jnp.concatenate([-values[..., half:], values[..., :half]], axis=-1)
    return values * cosine + turned * sine


def rms_scale(values, gain):
    return values * lax.rsqrt(jnp.mean(values * values, axis=-1, keepdims=True) + 1e-06) * gain


def body(hidden, modulation, w_qkv, w_out, qk_gain, stale, offsets, text_count, exponents):
    rows = hidden.shape[0]
    own_width = hidden.shape[1]
    heads = w_qkv.shape[1]
    head = w_qkv.shape[2] // 3
    whole, mods = (
        lax.all_gather(hidden, "tensor", axis=1, tiled=True),
        lax.all_gather(modulation, "tensor", axis=1, tiled=True),
    )
    xf = whole.astype(jnp.float32)
    centred = xf - jnp.mean(xf, axis=-1, keepdims=True)
    normed = centred * lax.rsqrt(jnp.mean(centred * centred, axis=-1, keepdims=True) + 1e-06)
    mods = mods.astype(jnp.float32)
    normed = (normed * (1.0 + mods[1]) + mods[0]).astype(jnp.bfloat16)
    qkv_flat = w_qkv.reshape(w_qkv.shape[0], heads * 3 * head)
    mixed = jnp.dot(
        normed,
        lax.all_gather(qkv_flat, "patch", axis=0, tiled=True),
        preferred_element_type=jnp.float32,
    )
    mixed = mixed.reshape(rows, heads, 3, head)
    query = rms_scale(mixed[:, :, 0], qk_gain[0])
    key_new = rms_scale(mixed[:, :, 1], qk_gain[1])
    value_new = mixed[:, :, 2]
    local = jnp.arange(rows, dtype=jnp.int32)
    positions = jnp.where(local < TXT_DEV, 0, offsets[0] + local - TXT_DEV).astype(jnp.float32)
    half = head // 2
    freqs = jnp.power(10000.0, -jnp.arange(half, dtype=jnp.float32) / half)
    angle = positions[:, None] * freqs[None, :]
    cosine = jnp.concatenate([jnp.cos(angle), jnp.cos(angle)], axis=-1)[:, None, :]
    sine = jnp.concatenate([jnp.sin(angle), jnp.sin(angle)], axis=-1)[:, None, :]
    query = rotate(query, cosine, sine).astype(jnp.bfloat16)
    key_new = rotate(key_new, cosine, sine)
    fresh = jnp.stack([key_new, value_new]).reshape(2, rows, heads * head)
    mine = lax.dynamic_slice_in_dim(stale, lax.axis_index("patch") * rows, rows, 1).astype(
        jnp.float32
    )
    limit = 127.0 * jnp.exp2(exponents[:, 0, :].astype(jnp.float32))
    limit = jnp.repeat(limit, head, axis=1)[:, None, :]
    change = jnp.clip(fresh - mine, -limit, limit).astype(jnp.bfloat16)
    changes = lax.all_gather(change, "patch", axis=1, tiled=True)
    total = stale.shape[1]
    keys = (stale[0].astype(jnp.float32) + changes[0].astype(jnp.float32)).astype(jnp.bfloat16)
    values = (stale[1].astype(jnp.float32) + changes[1].astype(jnp.float32)).astype(jnp.bfloat16)
    keys = keys.reshape(total, heads, head)
    values = values.reshape(total, heads, head)
    index = jnp.arange(total, dtype=jnp.int32)
    within = index % rows
    usable = (within >= TXT_DEV) | (index // rows * TXT_DEV + within < text_count[0])
    scale = head ** (-0.5)
    pieces = []
    for slot in range(heads):
        scores = (
            lax.dot_general(
                query[:, slot],
                keys[:, slot],
                (((1,), (1,)), ((), ())),
                preferred_element_type=jnp.float32,
            )
            * scale
        )
        scores = jnp.where(usable[None, :], scores, -1e30)
        peak = jnp.max(scores, axis=-1, keepdims=True)
        weights = jnp.exp(scores - peak)
        weights = (weights / jnp.sum(weights, axis=-1, keepdims=True)).astype(jnp.bfloat16)
        pieces.append(jnp.dot(weights, values[:, slot], preferred_element_type=jnp.float32))
    attended = jnp.concatenate(pieces, axis=-1).astype(jnp.bfloat16)
    projected = lax.dot_general(
        attended,
        lax.all_gather(w_out, "patch", axis=0, tiled=True),
        (((1,), (1,)), ((), ())),
        preferred_element_type=jnp.float32,
    )
    summed = lax.psum(projected.astype(jnp.bfloat16), "tensor").astype(jnp.float32)
    share = lax.dynamic_slice_in_dim(summed, lax.axis_index("tensor") * own_width, own_width, 1)
    gate = modulation[2].astype(jnp.float32)
    return (hidden.astype(jnp.float32) + gate * share).astype(jnp.bfloat16)


def solution(mesh):
    in_specs = (
        P(("groups", "patch"), "tensor"),
        P(None, "tensor"),
        P("patch", "tensor", None),
        P("patch", "tensor"),
        P(None, "tensor", None),
        P(None, "groups", "tensor"),
        P(("groups", "patch")),
        P("groups"),
        P(None, ("groups", "patch"), "tensor"),
    )
    out_specs = P(("groups", "patch"), "tensor")
    return jax.shard_map(body, mesh=mesh, in_specs=in_specs, out_specs=out_specs, check_vma=False)
```

profile of v0, /device:TPU:1, one launch (start us, length us, event | category | flops | bytes accessed | tf_op | source)
XLA Modules:
  0.0 191.1 jit_solution(11135200758820021268)
XLA Ops:
  6.5 2.6 %copy.22 = bf16[96,8,2,384]{3,1,2,0:T(8,128)(2,1)} copy(bf16[96,8,2,384]{3,2,1,0:T(2,128)(2,1)} %bitcast.62) | data formatting | bytes 2359296
  9.2 0.7 all-gather.5.cloned.1.call-update
  10.0 6.1 %all_gather.16 = bf16[3,3072]{1,0:T(4,128)(2,1)S(1)} all-gather(bf16[3,768]{1,0:T(4,128)(2,1)S(1)} %copy-done.2), channel_id=1, replica_groups=mesh['groups'=2,'patch'=4,'tensor'=4] {'tensor'}, dimensions={1}, use_global_device_ids=true | all-gather | bytes 23040 | tf_op jit(solution)/shard_map/all_gather | solution.py:26
  16.2 9.6 %all_gather.15 = bf16[144,3072]{1,0:T(8,128)(2,1)S(1)} all-gather(bf16[144,768]{1,0:T(8,128)(2,1)S(1)} %copy-done.1), channel_id=1, replica_groups=mesh['groups'=2,'patch'=4,'tensor'=4] {'tensor'}, dimensions={1}, use_global_device_ids=true | all-gather | bytes 1105920 | tf_op jit(solution)/shard_map/all_gather | solution.py:25
  26.0 0.4 fusion.2
  27.1 0.3 multiply_cosine_fusion
  28.6 72.3 %all-gather.3.cloned.1.call-done = bf16[3072,768]{1,0:T(8,128)(2,1)} async-done(((bf16[768,768]{1,0:T(8,128)(2,1)}), bf16[3072,768]{1,0:T(8,128)(2,1)}) %all-gather.3.cloned.1.call-update) | async-done | bytes 4718608 | tf_op jit(solution)/shard_map/all_gather | solution.py:36
  100.9 3.3 %fusion.8 = f32[144,768]{1,0:T(8,128)S(1)} fusion(bf16[3072,768]{1,0:T(8,128)(2,1)} %all-gather.3.cloned.1.call-done, bf16[144,3072]{1,0:T(8,128)(2,1)S(1)} %all_gather.15, f32[3072]{0:T(1024)S(1)} %bitcast.63, f32[3072]{0:T(1024)S(1)} %bitcast.64, f32[144]{0:T(256)S(1)} %add_rsqrt_fusion.2, f32[144]{0:T(256)S(1)} %broadcast_multiply_fusion), kind=kOutput, calls=%fused_computation.15 | convolution fusion | flops 682131456 | bytes 6071424 | tf_op jit(solution)/shard_map/dot_general | solution.py:34
  104.2 0.2 reshape.189
  104.5 1.1 slice_reduce_fusion.1
  105.5 0.2 multiply_reduce_fusion
  105.8 0.2 multiply_multiply_fusion
  106.0 0.2 fusion.19
  106.2 0.2 pad_maximum_fusion
  106.6 0.2 mul.214
  107.3 20.9 %all_gather.18 = bf16[2,576,256]{2,1,0:T(8,128)(2,1)S(1)} all-gather(bf16[2,144,256]{2,1,0:T(8,128)(2,1)S(1)} %fusion.18), channel_id=1, replica_groups=mesh['groups'=2,'patch'=4,'tensor'=4] {'patch'}, dimensions={1}, use_global_device_ids=true | all-gather | bytes 737280 | tf_op jit(solution)/shard_map/all_gather | solution.py:59
  128.5 0.2 multiply_reduce_fusion.1
  128.8 0.2 multiply_multiply_fusion.1
  129.0 0.2 slice_negate_fusion.1
  129.3 0.4 fusion.21
  129.8 0.4 fusion.51
  130.2 0.3 fusion.54
  130.5 0.2 fusion.14
  130.7 0.3 fusion.53
  131.1 0.2 fusion.15
  131.3 0.4 fusion.50
  131.7 0.3 convolution_convert_fusion.2
  132.0 0.3 convolution_convert_fusion.1
  132.3 13.4 %all-gather.5.cloned.1.call-done = bf16[3072,256]{1,0:T(8,128)(2,1)} async-done(((bf16[768,256]{1,0:T(8,128)(2,1)}), bf16[3072,256]{1,0:T(8,128)(2,1)}) %all-gather.5.cloned.1.call-update) | async-done | bytes 1572880 | tf_op jit(solution)/shard_map/all_gather | solution.py:88
  145.7 3.0 %convolution_convert_fusion = bf16[144,3072]{1,0:T(8,128)(2,1)} fusion(bf16[3072,256]{1,0:T(8,128)(2,1)} %all-gather.5.cloned.1.call-done, bf16[144,128]{1,0:T(8,128)(2,1)S(1)} %convolution_convert_fusion.1, bf16[144,128]{1,0:T(8,128)(2,1)S(1)} %convolution_convert_fusion.2), kind=kOutput, calls=%fused_computation | convolution fusion | flops 227082240 | bytes 2531328 | tf_op jit(solution)/shard_map/dot_general | solution.py:86
  148.8 34.1 %all-reduce.2.cloned.1.call-done = bf16[144,3072]{1,0:T(8,128)(2,1)} async-done(((bf16[144,3072]{1,0:T(8,128)(2,1)}), bf16[144,3072]{1,0:T(8,128)(2,1)}) %all-reduce.2.cloned.1.call-update) | async-done | bytes 884752 | tf_op jit(solution)/shard_map/psum | solution.py:92
  182.9 1.7 add_convert_fusion.2
  (47 shorter events, 2.0 us)
Async XLA Ops:
  6.5 94.3 %all-gather.3.cloned.1.call-start = ((), (), s32[]{:S(2)}) async-start(), calls=%async_computation | async-start | bytes 5898240 | tf_op jit(solution)/shard_map/all_gather | solution.py:36
  6.5 3.4 %copy-start.2 = (bf16[3,768]{1,0:T(4,128)(2,1)S(1)}, bf16[3,768]{1,0:T(4,128)(2,1)}, u32[]{:S(2)}) copy-start(bf16[3,768]{1,0:T(4,128)(2,1)} %param.10) | copy-start | bytes 13828
  6.5 9.5 %copy-start.4 = (s32[2,1,2]{2,1,0:T(1,128)S(1)}, s32[2,1,2]{2,1,0:T(1,128)}, u32[]{:S(2)}) copy-start(s32[2,1,2]{2,1,0:T(1,128)} %param.17) | copy-start | bytes 52
  6.5 9.6 %copy-start.1 = (bf16[144,768]{1,0:T(8,128)(2,1)S(1)}, bf16[144,768]{1,0:T(8,128)(2,1)}, u32[]{:S(2)}) copy-start(bf16[144,768]{1,0:T(8,128)(2,1)} %param.9) | copy-start | bytes 663556
  9.1 17.3 %copy-start.3 = (f32[2,2,128]{2,1,0:T(2,128)S(1)}, f32[2,2,128]{2,1,0:T(2,128)}, u32[]{:S(2)}) copy-start(f32[2,2,128]{2,1,0:T(2,128)} %param.13) | copy-start | bytes 6148
  9.2 136.6 %all-gather.5.cloned.1.call-start = ((), (), s32[]{:S(2)}) async-start(), calls=%async_computation.1 | async-start | bytes 1966080 | tf_op jit(solution)/shard_map/all_gather | solution.py:88
  9.9 173.0 %all-reduce.2.cloned.1.call-start = ((), (), s32[]{:S(2)}) async-start(), calls=%async_computation.2 | async-start | bytes 1769472 | tf_op jit(solution)/shard_map/psum | solution.py:92
  105.8 1.5 copy-start
Sparse Core Ops, SparseCore 0:
  9.3 91.5 all-gather.2
  102.4 43.2 all-gather.4
  148.9 33.9 all-reduce.1
where the time goes:
time: 193 us; the launch traced here: 191 us
  waiting for transfers between devices  120 us (62%)
  blocking collectives  36.6 us (19%)
  between operations  14.7 us (8%)
  matrix products  7.58 us (4%)
  local copies, waits for them, and re-layouts  6.11 us (3%)
  other arithmetic  5.51 us (3%)
    all_gather x1, waiting for transfers between devices, body(): lax.all_gather(qkv_flat, 'patch', axis=0, tiled=True)  72.3 us
    psum x1, waiting for transfers between devices, body(): lax.psum(projected.astype(jnp.bfloat16), 'tensor').astype(jnp.float32)  34.1 us
    all_gather x1, blocking collectives, body(): changes = lax.all_gather(change, 'patch', axis=1, tiled=True)  20.9 us
    all_gather x1, waiting for transfers between devices, body(): lax.all_gather(w_out, 'patch', axis=0, tiled=True)  13.4 us
    all_gather x1, blocking collectives, body(): lax.all_gather(hidden, 'tensor', axis=1, tiled=True)  9.6 us
    all_gather x1, blocking collectives, body(): lax.all_gather(modulation, 'tensor', axis=1, tiled=True)  6.06 us
  transfers between devices with their start and end apart: 3, of which 3 were waited for; matrix products, arithmetic and copies ran while one was open for 6% of the time, Pallas kernels for 0%

commit v1 on v0

--- a/solution.py
+++ b/solution.py
@@ -1,9 +1,17 @@
+import functools
+
+import numpy as np
 import jax
 import jax.numpy as jnp
 from jax import lax
+from jax.experimental import pallas as pl
+from jax.experimental.pallas import tpu as pltpu
 from jax.sharding import PartitionSpec as P
 
 TXT_DEV = 16
+F32 = jnp.float32
+BF16 = jnp.bfloat16
+MESH = pl.DeviceIdType.MESH
 
 
 def rotate(values, cosine, sine):
@@ -16,7 +24,7 @@
     return values * lax.rsqrt(jnp.mean(values * values, axis=-1, keepdims=True) + 1e-06) * gain
 
 
-def body(hidden, modulation, w_qkv, w_out, qk_gain, stale, offsets, text_count, exponents):
+def plain_body(hidden, modulation, w_qkv, w_out, qk_gain, stale, offsets, text_count, exponents):
     rows = hidden.shape[0]
     own_width = hidden.shape[1]
     heads = w_qkv.shape[1]
@@ -95,6 +103,361 @@
     return (hidden.astype(jnp.float32) + gate * share).astype(jnp.bfloat16)
 
 
+def kernel(
+    hidden, mods, w_qkv, w_out, gain, stale, freqs, offsets, text_count, exponents, out,
+    hbuf, modbuf, wbuf, wobuf, metasrc, meta, stbuf, normed, mixed, cosbuf, sinbuf, kv, att, abuf, res, landed,
+    h_send, h_recv, hf_send, m_send, m_recv, w_send, w_recv, wf_send, wo_send, wo_recv,
+    me_send, me_recv, st_send, st_recv, kv_send, kv_recv, a_send, a_recv, r_send, r_recv,
+):
+    g = lax.axis_index("groups")
+    z = lax.axis_index("patch")
+    t = lax.axis_index("tensor")
+    x = t // 2
+    c = t % 2
+    lead = z // 2
+    rows, width = hidden.shape
+    half_k = width // 2
+    head = stale.shape[2] // 2
+    mine = 2 * rows
+    leading = c == lead
+
+    def remote(src, dst, send, recv, device):
+        return pltpu.make_async_remote_copy(
+            src_ref=src, dst_ref=dst, send_sem=send, recv_sem=recv, device_id=device, device_id_type=MESH
+        )
+
+    sibling = (g, z, 2 * x + 1 - c)
+
+    def arrived(ref, sem):
+        remote(ref, ref, st_send.at[0], sem, sibling).wait_recv()
+
+    def left(ref, sem):
+        remote(ref, ref, sem, st_recv.at[0], sibling).wait_send()
+
+    modbuf[t, 0:3, :] = mods[...].astype(F32)
+    for hl in range(2):
+        for kind in range(2):
+            scale = jnp.exp2(jnp.full((1, head), exponents[kind, 0, hl], jnp.int32).astype(F32))
+            scale = jnp.floor(scale * 65536.0 + 0.5) * (1.0 / 65536.0)
+            metasrc[hl, kind : kind + 1, :] = 127.0 * scale
+            metasrc[hl, 2 + kind : 3 + kind, :] = gain[kind, hl : hl + 1, :]
+        metasrc[hl, 4:5, :] = jnp.full((1, head), offsets[0], jnp.int32).astype(F32)
+
+    barrier = pltpu.get_barrier_semaphore()
+    for dz in range(4):
+        for dt in range(4):
+            if dz or dt:
+                pl.semaphore_signal(
+                    barrier, inc=1, device_id=(g, (z + dz) % 4, (t + dt) % 4), device_id_type=MESH
+                )
+    for core in range(2):
+        pl.semaphore_signal(barrier, inc=1, device_id=(1 - g, z, 2 * x + core), device_id_type=MESH)
+    pl.semaphore_wait(barrier, 17)
+
+    target = z // 2
+    j_mine = z % 2
+
+    for hl in range(2):
+        zt = 2 * c + hl
+
+        @pl.when(zt != z)
+        def _():
+            remote(
+                w_qkv.at[pl.ds(g * half_k, half_k), pl.ds(hl * 3 * head, 3 * head)],
+                wbuf.at[z, g],
+                w_send.at[hl],
+                w_recv.at[z, g],
+                (g, zt, t),
+            ).start()
+            remote(metasrc.at[hl], meta.at[j_mine], me_send.at[hl], me_recv.at[j_mine],
+                   (g, zt, 2 * x + target)).start()
+
+    for d in range(1, 4):
+        remote(hidden, hbuf.at[j_mine, t], h_send.at[d], h_recv.at[j_mine, t],
+               (g, (z + d) % 4, 2 * x + target)).start()
+
+    @pl.when(c != target)
+    def _():
+        remote(hidden, hbuf.at[j_mine, t], h_send.at[0], h_recv.at[j_mine, t], sibling).start()
+
+    @pl.when(c == target)
+    def _():
+        hbuf[j_mine, t] = hidden[...]
+
+    for d in range(1, 4):
+        remote(modbuf.at[t], modbuf.at[t], m_send.at[d], m_recv.at[t], (g, z, (t + d) % 4)).start()
+
+    for hl in range(2):
+        @pl.when(jnp.logical_and(leading, z % 2 == hl))
+        def _():
+            for part in range(2):
+                remote(
+                    w_qkv.at[pl.ds(part * half_k, half_k), pl.ds(hl * 3 * head, 3 * head)],
+                    wbuf.at[z, part],
+                    w_send.at[2 + part],
+                    w_recv.at[z, part],
+                    sibling,
+                ).start()
+                wbuf[z, part] = w_qkv[pl.ds(part * half_k, half_k), pl.ds(hl * 3 * head, 3 * head)]
+            remote(
+                stale.at[:, pl.ds(pl.multiple_of((1 - c) * mine, 16), mine), pl.ds(hl * head, head)],
+                stbuf, st_send.at[0], st_recv.at[0], sibling,
+            ).start()
+            stbuf[...] = stale[:, pl.ds(pl.multiple_of(c * mine, 16), mine), pl.ds(hl * head, head)]
+            meta[hl] = metasrc[hl]
+
+    def line_slot(j, cs):
+        p = 2 * c + j
+        ts = 2 * x + cs
+
+        @pl.when(jnp.logical_not(jnp.logical_and(p == z, c == cs)))
+        def _():
+            arrived(hbuf.at[j, ts], h_recv.at[j, ts])
+
+        remote(hbuf.at[j, ts], hbuf.at[j, ts], hf_send.at[j, cs], h_recv.at[j, ts],
+               (g, z, 2 * (1 - x) + c)).start()
+
+    def weight_slot(d):
+        zs = (z + d) % 4
+
+        @pl.when(leading)
+        def _():
+            arrived(wbuf.at[zs, g], w_recv.at[zs, g])
+            for k, device in enumerate((
+                (1 - g, z, t), (1 - g, z, 2 * x + 1 - c), sibling,
+            )):
+                remote(wbuf.at[zs, g], wbuf.at[zs, g], wf_send.at[d, k], w_recv.at[zs, g], device).start()
+
+    weight_slot(1)
+    line_slot(0, 0)
+    line_slot(0, 1)
+    weight_slot(3)
+    line_slot(1, 0)
+    line_slot(1, 1)
+    weight_slot(2)
+
+    wobuf[t] = w_out[...]
+    for d in range(1, 4):
+        remote(w_out, wobuf.at[t], wo_send.at[d], wo_recv.at[t], (g, z, (t + d) % 4)).start()
+
+    place = lax.broadcasted_iota(jnp.int32, (rows, head), 0)
+    lane = lax.broadcasted_iota(jnp.int32, (rows, head), 1)
+    for j in range(2):
+        @pl.when(jnp.logical_not(jnp.logical_and(leading, z % 2 == j)))
+        def _():
+            arrived(meta.at[j], me_recv.at[j])
+
+        positions = jnp.where(place < TXT_DEV, 0.0, meta[j, 4:5, :] + (place - TXT_DEV).astype(F32))
+        angle = positions * freqs[...]
+        cosbuf[pl.ds(j * rows, rows), :] = jnp.cos(angle)
+        sine = jnp.sin(angle)
+        sinbuf[pl.ds(j * rows, rows), :] = jnp.where(lane < head // 2, -sine, sine)
+
+    for d in range(1, 4):
+        arrived(modbuf.at[(t + d) % 4], m_recv.at[(t + d) % 4])
+    features = 4 * width
+    for j in range(2):
+        for cs in range(2):
+            arrived(hbuf.at[j, 2 * (1 - x) + cs], h_recv.at[j, 2 * (1 - x) + cs])
+
+        @pl.loop(0, rows // 16)
+        def _(i):
+            at = pl.ds(pl.multiple_of(i * 16, 16), 16)
+            xs = [hbuf[j, k, at, :].astype(F32) for k in range(4)]
+            total = sum(jnp.sum(v, axis=-1, keepdims=True) for v in xs)
+            mean = total * (1.0 / features)
+            xs = [v - mean for v in xs]
+            total = sum(jnp.sum(v * v, axis=-1, keepdims=True) for v in xs)
+            inverse = lax.rsqrt(total * (1.0 / features) + 1e-06)
+            to = pl.ds(pl.multiple_of(j * rows + i * 16, 16), 16)
+            for k in range(4):
+                value = xs[k] * inverse * (1.0 + modbuf[k, 1:2, :]) + modbuf[k, 0:1, :]
+                normed[to, pl.ds(k * width, width)] = value.astype(BF16)
+
+    for zs in range(4):
+        for part in range(2):
+            own = jnp.logical_and(leading, jnp.logical_or(zs == z, g == part))
+
+            @pl.when(jnp.logical_not(own))
+            def _():
+                arrived(wbuf.at[zs, part], w_recv.at[zs, part])
+
+            value = jnp.dot(
+                normed[:, pl.ds(zs * width + part * half_k, half_k)], wbuf[zs, part],
+                preferred_element_type=F32,
+            )
+            if zs or part:
+                mixed[...] += value
+            else:
+                mixed[...] = value
+
+    @pl.when(jnp.logical_not(leading))
+    def _():
+        arrived(stbuf, st_recv.at[0])
+
+    def rms(values, row):
+        root = lax.rsqrt(jnp.mean(values * values, axis=-1, keepdims=True) + 1e-06)
+        return values * root * meta[0, row : row + 1, :]
+
+    def turn(values):
+        return values * cosbuf[...] + pltpu.roll(values, head // 2, 1) * sinbuf[...]
+
+    second = lax.broadcasted_iota(jnp.int32, (mine, head), 0) >= rows
+    ours = pl.ds(pl.multiple_of(c * mine, 16), mine)
+    key_new = turn(rms(mixed[:, head : 2 * head], 3))
+    for kind, fresh in enumerate((key_new, mixed[:, 2 * head : 3 * head])):
+        limit = jnp.where(second, meta[1, kind : kind + 1, :], meta[0, kind : kind + 1, :])
+        old = stbuf[kind].astype(F32)
+        change = jnp.clip(fresh - old, -limit, limit).astype(BF16)
+        kv[kind, ours, :] = (old + change.astype(F32)).astype(BF16)
+    remote(kv.at[:, ours, :], kv.at[:, ours, :], kv_send.at[0], kv_recv.at[0], sibling).start()
+    query = turn(rms(mixed[:, 0:head], 2)).astype(BF16)
+    theirs = pl.ds(pl.multiple_of((1 - c) * mine, 16), mine)
+    arrived(kv.at[:, theirs, :], kv_recv.at[0])
+
+    keys = kv[0]
+    values = kv[1]
+    index = lax.broadcasted_iota(jnp.int32, (1, 2 * mine), 1)
+    within = index % rows
+    usable = (within >= TXT_DEV) | (index // rows * TXT_DEV + within < text_count[0])
+    my_head = 4 * x + z
+    for j in range(2):
+        scores = lax.dot_general(
+            query[j * rows : (j + 1) * rows], keys, (((1,), (1,)), ((), ())), preferred_element_type=F32
+        ) * (head ** (-0.5))
+        scores = jnp.where(usable, scores, -1e30)
+        peak = jnp.max(scores, axis=-1, keepdims=True)
+        weights = jnp.exp(scores - peak)
+        weights = (weights / jnp.sum(weights, axis=-1, keepdims=True)).astype(BF16)
+        att[j] = jnp.dot(weights, values, preferred_element_type=F32).astype(BF16)
+        for d in range(1, 4):
+            remote(att.at[j], abuf.at[my_head], a_send.at[j, d], a_recv.at[my_head],
+                   (g, (z + d) % 4, 2 * j + c)).start()
+
+        @pl.when(x == j)
+        def _():
+            abuf[my_head] = att[j]
+
+        @pl.when(x != j)
+        def _():
+            remote(att.at[j], abuf.at[my_head], a_send.at[j, 0], a_recv.at[my_head], (g, z, 2 * j + c)).start()
+
+    for d in range(1, 4):
+        arrived(wobuf.at[(t + d) % 4], wo_recv.at[(t + d) % 4])
+    for h in range(8):
+        @pl.when(h != my_head)
+        def _():
+            arrived(abuf.at[h], a_recv.at[h])
+
+    total = None
+    for k in range(4):
+        pair = jnp.concatenate([abuf[2 * k], abuf[2 * k + 1]], axis=-1)
+        value = lax.dot_general(pair, wobuf[k], (((1,), (1,)), ((), ())), preferred_element_type=F32)
+        total = value if total is None else total + value
+    res[...] = (hbuf[x, z].astype(F32) + modbuf[z, 2:3, :] * total).astype(BF16)
+    owner = 2 * c + x
+    home = jnp.logical_and(owner == z, z == t)
+
+    @pl.when(home)
+    def _():
+        landed[...] = res[...]
+
+    @pl.when(jnp.logical_not(home))
+    def _():
+        remote(res, landed, r_send.at[0], r_recv.at[0], (g, owner, z)).start()
+
+    from_self = jnp.logical_and(t == z, 2 * (z % 2) + z // 2 == t)
+
+    @pl.when(jnp.logical_not(from_self))
+    def _():
+        arrived(landed, r_recv.at[0])
+
+    out[...] = landed[...]
+
+    for hl in range(2):
+        @pl.when(2 * c + hl != z)
+        def _():
+            left(wbuf.at[z, g], w_send.at[hl])
+            left(metasrc.at[hl], me_send.at[hl])
+    for d in range(1, 4):
+        left(hidden, h_send.at[d])
+        left(modbuf.at[t], m_send.at[d])
+        left(w_out, wo_send.at[d])
+        for j in range(2):
+            left(att.at[j], a_send.at[j, d])
+
+    @pl.when(c != target)
+    def _():
+        left(hidden, h_send.at[0])
+
+    @pl.when(leading)
+    def _():
+        for part in range(2):
+            left(wbuf.at[z, part], w_send.at[2 + part])
+        left(stbuf, st_send.at[0])
+        for d in range(1, 4):
+            for k in range(3):
+                left(wbuf.at[(z + d) % 4, g], wf_send.at[d, k])
+
+    for j in range(2):
+        for cs in range(2):
+            left(hbuf.at[j, 2 * x + cs], hf_send.at[j, cs])
+
+        @pl.when(x != j)
+        def _():
+            left(att.at[j], a_send.at[j, 0])
+    left(kv.at[:, ours, :], kv_send.at[0])
+
+    @pl.when(jnp.logical_not(home))
+    def _():
+        left(res, r_send.at[0])
+
+
+def body(hidden, modulation, w_qkv, w_out, qk_gain, stale, offsets, text_count, exponents):
+    rows, width = hidden.shape
+    head = w_qkv.shape[2] // 3
+    half = head // 2
+    freqs = np.power(10000.0, -np.arange(half) / half).astype(np.float32)
+    freqs = jnp.asarray(np.concatenate([freqs, freqs])[None])
+    dma = pltpu.SemaphoreType.DMA
+    vmem = pl.BlockSpec(memory_space=pltpu.VMEM)
+    smem = pl.BlockSpec(memory_space=pltpu.SMEM)
+    return pl.pallas_call(
+        kernel,
+        out_shape=jax.ShapeDtypeStruct((rows, width), BF16),
+        in_specs=[vmem] * 7 + [smem] * 3,
+        out_specs=vmem,
+        scratch_shapes=[
+            pltpu.VMEM((2, 4, rows, width), BF16),
+            pltpu.VMEM((4, 8, width), F32),
+            pltpu.VMEM((4, 2, width // 2, 3 * head), BF16),
+            pltpu.VMEM((4, width, 2 * head), BF16),
+            pltpu.VMEM((2, 8, head), F32),
+            pltpu.VMEM((2, 8, head), F32),
+            pltpu.VMEM((2, 2 * rows, head), BF16),
+            pltpu.VMEM((2 * rows, 4 * width), BF16),
+            pltpu.VMEM((2 * rows, 3 * head), F32),
+            pltpu.VMEM((2 * rows, head), F32),
+            pltpu.VMEM((2 * rows, head), F32),
+            pltpu.VMEM((2, 4 * rows, head), BF16),
+            pltpu.VMEM((2, rows, head), BF16),
+            pltpu.VMEM((8, rows, head), BF16),
+            pltpu.VMEM((rows, width), BF16),
+            pltpu.VMEM((rows, width), BF16),
+            dma((4,)), dma((2, 4)), dma((2, 2)), dma((4,)), dma((4,)),
+            dma((4,)), dma((4, 2)), dma((4, 3)), dma((4,)), dma((4,)),
+            dma((2,)), dma((2,)), dma((1,)), dma((1,)), dma((1,)), dma((1,)),
+            dma((2, 4)), dma((8,)), dma((1,)), dma((1,)),
+        ],
+        compiler_params=pltpu.CompilerParams(
+            collective_id=0, has_side_effects=True, vmem_limit_bytes=40 * 2**20
+        ),
+    )(
+        hidden, modulation, w_qkv.reshape(w_qkv.shape[0], -1), w_out, qk_gain, stale, freqs,
+        offsets, text_count, exponents,
+    )
+
+
 def solution(mesh):
     in_specs = (
         P(("groups", "patch"), "tensor"),
@@ -108,4 +471,7 @@
         P(None, ("groups", "patch"), "tensor"),
     )
     out_specs = P(("groups", "patch"), "tensor")
-    return jax.shard_map(body, mesh=mesh, in_specs=in_specs, out_specs=out_specs, check_vma=False)
+    small = (mesh.shape["groups"], mesh.shape["patch"], mesh.shape["tensor"]) == (2, 4, 4)
+    return jax.shard_map(
+        body if small else plain_body, mesh=mesh, in_specs=in_specs, out_specs=out_specs, check_vma=False
+    )

time: 193 us -> 86.7 us (0.45)
  waiting for transfers between devices: 120 us -> 0 us
  Pallas kernels: 0 us -> 82.8 us
  blocking collectives: 36.6 us -> 0 us
  between operations: 14.7 us -> 1.42 us
  matrix products: 7.58 us -> 0 us
  other arithmetic: 5.51 us -> 0 us
  local copies, waits for them, and re-layouts: 6.11 us -> 2.3 us
    all_gather x2 -> x0, waiting for transfers between devices: 85.6 us -> none  [the longest x1 72.3 us: body(): lax.all_gather(qkv_flat, 'patch', axis=0, tiled=True)]
    pallas_call x0 -> x1, Pallas kernels: none -> 82.8 us  [body(): pl.pallas_call(kernel, out_shape=jax.ShapeDtypeStruct((rows, width), BF16...]
    all_gather x3 -> x0, blocking collectives: 36.6 us -> none  [the longest x1 20.9 us: body(): changes = lax.all_gather(change, 'patch', axis=1, tiled=True)]
    psum x1 -> x0, waiting for transfers between devices: 34.1 us -> none  [body(): lax.psum(projected.astype(jnp.bfloat16), 'tensor').astype(jnp.float32)]
    dot_general x6 -> x0, matrix products: 7.58 us -> none  [the longest x1 3.33 us: body(): jnp.dot(normed, lax.all_gather(qkv_flat, 'patch', axis=0, tiled=True), pr...]
    convert_element_type x6 -> x0, other arithmetic: 2.29 us -> none  [the longest x1 1.69 us: body(): return (hidden.astype(jnp.float32) + gate * share).astype(jnp.bfloat16)]
    slice x5 -> x0, local copies, waits for them, and re-layouts: 2 us -> none  [the longest x1 1.06 us: body(): key_new = rms_scale(mixed[:, :, 1], qk_gain[1])]
  transfers between devices with their start and end apart: 3 -> 0, of which waited for: 3 -> 0; matrix products, arithmetic and copies ran while one was open for 6% -> 0% of each run, Pallas kernels for 0% -> 0%
where the time goes in v1:
time: 86.7 us; the launch traced here: 86.5 us
  Pallas kernels  82.8 us (96%)
  local copies, waits for them, and re-layouts  2.3 us (3%)
  between operations  1.42 us (2%)
    pallas_call x1, Pallas kernels, body(): pl.pallas_call(kernel, out_shape=jax.ShapeDtypeStruct((rows, width), BF16...  82.8 us
    unnamed x16, local copies, waits for them, and re-layouts  2.3 us

profile of v1, /device:TPU:1, one launch (start us, length us, event | category | flops | bytes accessed | tf_op | source)
XLA Modules:
  0.0 86.5 jit_solution(16807095848786375700)
XLA Ops:
  1.3 0.0 copy-start
  1.3 0.0 copy-start.1
  1.3 0.0 copy-start.2
  1.3 0.0 copy-start.3
  1.3 0.0 copy-start.4
  1.3 0.0 copy-start.5
  1.4 0.0 copy-start.6
  1.4 1.6 %copy.11 = bf16[96,8,2,384]{3,1,2,0:T(8,128)(2,1)S(1)} copy(bf16[96,8,2,384]{3,2,1,0:T(2,128)(2,1)} %bitcast.3) | data formatting | bytes 2359296
  3.0 0.0 copy-done
  3.0 0.0 copy-done.1
  3.0 0.0 copy-done.2
  3.0 0.0 copy-done.3
  3.0 0.0 copy-done.4
  3.0 0.0 copy-done.5
  3.0 0.0 copy-done.6
  3.0 82.8 %shard_map.100 = bf16[144,768]{1,0:T(8,128)(2,1)S(1)} custom-call(bf16[144,768]{1,0:T(8,128)(2,1)S(1)} %copy-done.2, bf16[3,768]{1,0:T(4,128)(2,1)S(1)} %copy-done.3, bf16[768,768]{1,0:T(8,128)(2,1)S(1)} %bitcast.2, bf16[768,256]{1,0:T(8,128)(2,1)S(1)} %copy-done.1, f32[2,2,128]{2,1,0:T(2,128)S(1)} %copy-done.4, bf16[2,576,256]{2,1,0:T(8,128)(2,1)S(1)} %copy-done, ...), custom_call_target="tpu_custom_call" | custom-call | tf_op jit(solution)/shard_map/pallas_call | solution.py:425
  85.9 0.7 copy.15
Async XLA Ops:
  1.3 1.7 %copy-start = (bf16[2,576,256]{2,1,0:T(8,128)(2,1)S(1)}, bf16[2,576,256]{2,1,0:T(8,128)(2,1)}, u32[]{:S(2)}) copy-start(bf16[2,576,256]{2,1,0:T(8,128)(2,1)} %stale.1) | copy-start | bytes 1769476
  1.3 1.7 %copy-start.1 = (bf16[768,256]{1,0:T(8,128)(2,1)S(1)}, bf16[768,256]{1,0:T(8,128)(2,1)}, u32[]{:S(2)}) copy-start(bf16[768,256]{1,0:T(8,128)(2,1)} %w_out.1) | copy-start | bytes 1179652
  1.3 1.7 %copy-start.2 = (bf16[144,768]{1,0:T(8,128)(2,1)S(1)}, bf16[144,768]{1,0:T(8,128)(2,1)}, u32[]{:S(2)}) copy-start(bf16[144,768]{1,0:T(8,128)(2,1)} %hidden.1) | copy-start | bytes 663556
  1.3 1.7 %copy-start.3 = (bf16[3,768]{1,0:T(4,128)(2,1)S(1)}, bf16[3,768]{1,0:T(4,128)(2,1)}, u32[]{:S(2)}) copy-start(bf16[3,768]{1,0:T(4,128)(2,1)} %mods.1) | copy-start | bytes 13828
  1.3 1.7 %copy-start.4 = (f32[2,2,128]{2,1,0:T(2,128)S(1)}, f32[2,2,128]{2,1,0:T(2,128)}, u32[]{:S(2)}) copy-start(f32[2,2,128]{2,1,0:T(2,128)} %gain.1) | copy-start | bytes 6148
  1.3 1.7 %copy-start.5 = (s32[2,1,2]{2,1,0:T(1,128)S(1)}, s32[2,1,2]{2,1,0:T(1,128)}, u32[]{:S(2)}) copy-start(s32[2,1,2]{2,1,0:T(1,128)} %exponents.1) | copy-start | bytes 52
  1.4 1.7 %copy-start.6 = (f32[1,128]{1,0:T(1,128)S(1)}, f32[1,128]{1,0:T(1,128)}, u32[]{:S(2)}) copy-start(f32[1,128]{1,0:T(1,128)} %constant.2.clone.freqs) | copy-start | bytes 1540

commit v2 on v1

--- a/solution.py
+++ b/solution.py
@@ -12,6 +12,7 @@
 F32 = jnp.float32
 BF16 = jnp.bfloat16
 MESH = pl.DeviceIdType.MESH
+CHUNKS = 3
 
 
 def rotate(values, cosine, sine):
@@ -106,7 +107,7 @@
 def kernel(
     hidden, mods, w_qkv, w_out, gain, stale, freqs, offsets, text_count, exponents, out,
     hbuf, modbuf, wbuf, wobuf, metasrc, meta, stbuf, normed, mixed, cosbuf, sinbuf, kv, att, abuf, res, landed,
-    h_send, h_recv, hf_send, m_send, m_recv, w_send, w_recv, wf_send, wo_send, wo_recv,
+    h_send, h_recv, hf_send, m_send, m_recv, w_send, w_recv, wl_send, wf_send, wo_send, wo_recv,
     me_send, me_recv, st_send, st_recv, kv_send, kv_recv, a_send, a_recv, r_send, r_recv,
 ):
     g = lax.axis_index("groups")
@@ -116,7 +117,8 @@
     c = t % 2
     lead = z // 2
     rows, width = hidden.shape
-    half_k = width // 2
+    quarter = width // 4
+    chunk = rows // CHUNKS
     head = stale.shape[2] // 2
     mine = 2 * rows
     leading = c == lead
@@ -150,55 +152,65 @@
                 pl.semaphore_signal(
                     barrier, inc=1, device_id=(g, (z + dz) % 4, (t + dt) % 4), device_id_type=MESH
                 )
-    for core in range(2):
-        pl.semaphore_signal(barrier, inc=1, device_id=(1 - g, z, 2 * x + core), device_id_type=MESH)
-    pl.semaphore_wait(barrier, 17)
+    pl.semaphore_signal(barrier, inc=1, device_id=(1 - g, z, t), device_id_type=MESH)
+    pl.semaphore_wait(barrier, 16)
 
     target = z // 2
     j_mine = z % 2
 
+    def part_of(j, ts, k):
+        return hbuf.at[j, ts, pl.ds(k * chunk, chunk)]
+
+    for k in range(CHUNKS):
+        piece = hidden.at[pl.ds(k * chunk, chunk)]
+        place = part_of(j_mine, t, k)
+        got = h_recv.at[j_mine, t, k]
+
+        @pl.when(z < 3)
+        def _():
+            remote(piece, place, h_send.at[0, k], got, (g, z + 1, 2 * x + target)).start()
+
+        @pl.when(z > 0)
+        def _():
+            remote(piece, place, h_send.at[1, k], got, (g, z - 1, 2 * x + target)).start()
+
+        remote(piece, place, h_send.at[2, k], got, (g, z, 2 * (1 - x) + target)).start()
+
+        @pl.when(c != target)
+        def _():
+            remote(piece, place, h_send.at[3, k], got, sibling).start()
+
     for hl in range(2):
         zt = 2 * c + hl
 
         @pl.when(zt != z)
         def _():
-            remote(
-                w_qkv.at[pl.ds(g * half_k, half_k), pl.ds(hl * 3 * head, 3 * head)],
-                wbuf.at[z, g],
-                w_send.at[hl],
-                w_recv.at[z, g],
-                (g, zt, t),
-            ).start()
+            for core in range(2):
+                remote(
+                    w_qkv.at[pl.ds((2 * g + core) * quarter, quarter), pl.ds(hl * 3 * head, 3 * head)],
+                    wbuf.at[z, 2 * g + core],
+                    w_send.at[hl, core],
+                    w_recv.at[z, 2 * g + core],
+                    (g, zt, 2 * x + core),
+                ).start()
             remote(metasrc.at[hl], meta.at[j_mine], me_send.at[hl], me_recv.at[j_mine],
                    (g, zt, 2 * x + target)).start()
 
     for d in range(1, 4):
-        remote(hidden, hbuf.at[j_mine, t], h_send.at[d], h_recv.at[j_mine, t],
-               (g, (z + d) % 4, 2 * x + target)).start()
-
-    @pl.when(c != target)
-    def _():
-        remote(hidden, hbuf.at[j_mine, t], h_send.at[0], h_recv.at[j_mine, t], sibling).start()
-
-    @pl.when(c == target)
-    def _():
-        hbuf[j_mine, t] = hidden[...]
-
-    for d in range(1, 4):
         remote(modbuf.at[t], modbuf.at[t], m_send.at[d], m_recv.at[t], (g, z, (t + d) % 4)).start()
 
     for hl in range(2):
         @pl.when(jnp.logical_and(leading, z % 2 == hl))
         def _():
-            for part in range(2):
+            for part in range(4):
                 remote(
-                    w_qkv.at[pl.ds(part * half_k, half_k), pl.ds(hl * 3 * head, 3 * head)],
+                    w_qkv.at[pl.ds(part * quarter, quarter), pl.ds(hl * 3 * head, 3 * head)],
                     wbuf.at[z, part],
-                    w_send.at[2 + part],
+                    wl_send.at[part],
                     w_recv.at[z, part],
                     sibling,
                 ).start()
-                wbuf[z, part] = w_qkv[pl.ds(part * half_k, half_k), pl.ds(hl * 3 * head, 3 * head)]
+                wbuf[z, part] = w_qkv[pl.ds(part * quarter, quarter), pl.ds(hl * 3 * head, 3 * head)]
             remote(
                 stale.at[:, pl.ds(pl.multiple_of((1 - c) * mine, 16), mine), pl.ds(hl * head, head)],
                 stbuf, st_send.at[0], st_recv.at[0], sibling,
@@ -206,39 +218,77 @@
             stbuf[...] = stale[:, pl.ds(pl.multiple_of(c * mine, 16), mine), pl.ds(hl * head, head)]
             meta[hl] = metasrc[hl]
 
-    def line_slot(j, cs):
+    @pl.when(c == target)
+    def _():
+        hbuf[j_mine, t] = hidden[...]
+
+    half_out = width // 2
+    across = 2 * (1 - x) + c
+
+    def send_out():
+        remote(
+            w_out.at[pl.ds(g * half_out, half_out)], wobuf.at[t, g], wo_send.at[0], wo_recv.at[t, g],
+            (g, z, across),
+        ).start()
+        for part in range(2):
+            remote(
+                w_out.at[pl.ds(part * half_out, half_out)], wobuf.at[t, part], wo_send.at[1 + part],
+                wo_recv.at[t, part], sibling,
+            ).start()
+            wobuf[t, part] = w_out[pl.ds(part * half_out, half_out)]
+
+    def pass_out():
+        slot, got = wobuf.at[across, g], wo_recv.at[across, g]
+        arrived(slot, got)
+        remote(slot, slot, wo_send.at[3], got, (1 - g, z, t)).start()
+        remote(slot, slot, wo_send.at[4], got, sibling).start()
+
+    def pass_out_far():
+        slot, got = wobuf.at[across, 1 - g], wo_recv.at[across, 1 - g]
+        arrived(slot, got)
+        remote(slot, slot, wo_send.at[5], got, sibling).start()
+
+    first_j = jnp.where(c == 0, jnp.where(z == 0, 0, 1), jnp.where(z == 3, 1, 0))
+
+    def pass_hidden(order):
+        j = first_j if order == 0 else 1 - first_j
         p = 2 * c + j
-        ts = 2 * x + cs
-
-        @pl.when(jnp.logical_not(jnp.logical_and(p == z, c == cs)))
-        def _():
-            arrived(hbuf.at[j, ts], h_recv.at[j, ts])
-
-        remote(hbuf.at[j, ts], hbuf.at[j, ts], hf_send.at[j, cs], h_recv.at[j, ts],
-               (g, z, 2 * (1 - x) + c)).start()
-
-    def weight_slot(d):
+        onward = jnp.where(z > p, z + 1, z - 1)
+
+        @pl.when(p != z)
+        def _():
+            for k in range(CHUNKS):
+                for cs in range(2):
+                    slot, got = part_of(j, 2 * x + cs, k), h_recv.at[j, 2 * x + cs, k]
+                    arrived(slot, got)
+
+                    @pl.when(jnp.logical_and(onward >= 0, onward < 4))
+                    def _():
+                        remote(slot, slot, hf_send.at[order, cs, k, 0], got, (g, (onward + 4) % 4, t)).start()
+
+                    remote(slot, slot, hf_send.at[order, cs, k, 1], got, (g, z, across)).start()
+
+    def pass_weight(d):
         zs = (z + d) % 4
-
-        @pl.when(leading)
-        def _():
-            arrived(wbuf.at[zs, g], w_recv.at[zs, g])
-            for k, device in enumerate((
-                (1 - g, z, t), (1 - g, z, 2 * x + 1 - c), sibling,
-            )):
-                remote(wbuf.at[zs, g], wbuf.at[zs, g], wf_send.at[d, k], w_recv.at[zs, g], device).start()
-
-    weight_slot(1)
-    line_slot(0, 0)
-    line_slot(0, 1)
-    weight_slot(3)
-    line_slot(1, 0)
-    line_slot(1, 1)
-    weight_slot(2)
-
-    wobuf[t] = w_out[...]
-    for d in range(1, 4):
-        remote(w_out, wobuf.at[t], wo_send.at[d], wo_recv.at[t], (g, z, (t + d) % 4)).start()
+        slot, got = wbuf.at[zs, 2 * g + c], w_recv.at[zs, 2 * g + c]
+        arrived(slot, got)
+        remote(slot, slot, wf_send.at[d, 0], got, (1 - g, z, t)).start()
+        remote(slot, slot, wf_send.at[d, 1], got, sibling).start()
+
+    def pass_weight_far(d):
+        zs = (z + d) % 4
+        slot, got = wbuf.at[zs, 2 * (1 - g) + c], w_recv.at[zs, 2 * (1 - g) + c]
+        arrived(slot, got)
+        remote(slot, slot, wf_send.at[d, 2], got, sibling).start()
+
+    pass_hidden(0)
+    pass_weight(1)
+    pass_weight(3)
+    pass_hidden(1)
+    pass_weight(2)
+    send_out()
+    for d in (1, 3, 2):
+        pass_weight_far(d)
 
     place = lax.broadcasted_iota(jnp.int32, (rows, head), 0)
     lane = lax.broadcasted_iota(jnp.int32, (rows, head), 1)
@@ -257,8 +307,13 @@
         arrived(modbuf.at[(t + d) % 4], m_recv.at[(t + d) % 4])
     features = 4 * width
     for j in range(2):
-        for cs in range(2):
-            arrived(hbuf.at[j, 2 * (1 - x) + cs], h_recv.at[j, 2 * (1 - x) + cs])
+        for k in range(CHUNKS):
+            for cs in range(2):
+                arrived(part_of(j, 2 * (1 - x) + cs, k), h_recv.at[j, 2 * (1 - x) + cs, k])
+
+            @pl.when(z == 2 * c + j)
+            def _():
+                arrived(part_of(j, 2 * x + 1 - c, k), h_recv.at[j, 2 * x + 1 - c, k])
 
         @pl.loop(0, rows // 16)
         def _(i):
@@ -275,21 +330,25 @@
                 normed[to, pl.ds(k * width, width)] = value.astype(BF16)
 
     for zs in range(4):
-        for part in range(2):
-            own = jnp.logical_and(leading, jnp.logical_or(zs == z, g == part))
-
-            @pl.when(jnp.logical_not(own))
+        for core in range(2):
+            quarter_at = 2 * core + 1 - c
+
+            @pl.when(jnp.logical_not(jnp.logical_and(leading, zs == z)))
             def _():
-                arrived(wbuf.at[zs, part], w_recv.at[zs, part])
-
-            value = jnp.dot(
-                normed[:, pl.ds(zs * width + part * half_k, half_k)], wbuf[zs, part],
-                preferred_element_type=F32,
-            )
-            if zs or part:
-                mixed[...] += value
-            else:
-                mixed[...] = value
+                arrived(wbuf.at[zs, quarter_at], w_recv.at[zs, quarter_at])
+
+            @pl.when(jnp.logical_and(jnp.logical_not(leading), zs == z))
+            def _():
+                arrived(wbuf.at[zs, 2 * core + c], w_recv.at[zs, 2 * core + c])
+
+        value = jnp.dot(
+            normed[:, pl.ds(zs * width, width)], wbuf[zs].reshape(width, 3 * head), preferred_element_type=F32
+        )
+        if zs:
+            mixed[...] += value
+        else:
+            mixed[...] = value
+    pass_out()
 
     @pl.when(jnp.logical_not(leading))
     def _():
@@ -312,6 +371,7 @@
         kv[kind, ours, :] = (old + change.astype(F32)).astype(BF16)
     remote(kv.at[:, ours, :], kv.at[:, ours, :], kv_send.at[0], kv_recv.at[0], sibling).start()
     query = turn(rms(mixed[:, 0:head], 2)).astype(BF16)
+    pass_out_far()
     theirs = pl.ds(pl.multiple_of((1 - c) * mine, 16), mine)
     arrived(kv.at[:, theirs, :], kv_recv.at[0])
 
@@ -342,8 +402,9 @@
         def _():
             remote(att.at[j], abuf.at[my_head], a_send.at[j, 0], a_recv.at[my_head], (g, z, 2 * j + c)).start()
 
-    for d in range(1, 4):
-        arrived(wobuf.at[(t + d) % 4], wo_recv.at[(t + d) % 4])
+    for part in range(2):
+        for ts in (2 * x + 1 - c, 2 * (1 - x) + 1 - c):
+            arrived(wobuf.at[ts, part], wo_recv.at[ts, part])
     for h in range(8):
         @pl.when(h != my_head)
         def _():
@@ -352,7 +413,7 @@
     total = None
     for k in range(4):
         pair = jnp.concatenate([abuf[2 * k], abuf[2 * k + 1]], axis=-1)
-        value = lax.dot_general(pair, wobuf[k], (((1,), (1,)), ((), ())), preferred_element_type=F32)
+        value = lax.dot_general(pair, wobuf[k].reshape(width, 2 * head), (((1,), (1,)), ((), ())), preferred_element_type=F32)
         total = value if total is None else total + value
     res[...] = (hbuf[x, z].astype(F32) + modbuf[z, 2:3, :] * total).astype(BF16)
     owner = 2 * c + x
@@ -377,32 +438,59 @@
     for hl in range(2):
         @pl.when(2 * c + hl != z)
         def _():
-            left(wbuf.at[z, g], w_send.at[hl])
+            for core in range(2):
+                left(wbuf.at[z, 2 * g + core], w_send.at[hl, core])
             left(metasrc.at[hl], me_send.at[hl])
     for d in range(1, 4):
-        left(hidden, h_send.at[d])
         left(modbuf.at[t], m_send.at[d])
-        left(w_out, wo_send.at[d])
+        for k in range(2):
+            left(wbuf.at[(z + d) % 4, 2 * g + c], wf_send.at[d, k])
+        left(wbuf.at[(z + d) % 4, 2 * (1 - g) + c], wf_send.at[d, 2])
         for j in range(2):
             left(att.at[j], a_send.at[j, d])
-
-    @pl.when(c != target)
-    def _():
-        left(hidden, h_send.at[0])
+    for k in range(6):
+        left(wobuf.at[t, 0], wo_send.at[k])
+    for k in range(CHUNKS):
+        piece = hidden.at[pl.ds(k * chunk, chunk)]
+
+        @pl.when(z < 3)
+        def _():
+            left(piece, h_send.at[0, k])
+
+        @pl.when(z > 0)
+        def _():
+            left(piece, h_send.at[1, k])
+
+        left(piece, h_send.at[2, k])
+
+        @pl.when(c != target)
+        def _():
+            left(piece, h_send.at[3, k])
 
     @pl.when(leading)
     def _():
-        for part in range(2):
-            left(wbuf.at[z, part], w_send.at[2 + part])
+        for part in range(4):
+            left(wbuf.at[z, part], wl_send.at[part])
         left(stbuf, st_send.at[0])
-        for d in range(1, 4):
-            for k in range(3):
-                left(wbuf.at[(z + d) % 4, g], wf_send.at[d, k])
+
+    for order in range(2):
+        j = first_j if order == 0 else 1 - first_j
+        p = 2 * c + j
+        onward = jnp.where(z > p, z + 1, z - 1)
+
+        @pl.when(p != z)
+        def _():
+            for k in range(CHUNKS):
+                for cs in range(2):
+                    slot = part_of(j, 2 * x + cs, k)
+
+                    @pl.when(jnp.logical_and(onward >= 0, onward < 4))
+                    def _():
+                        left(slot, hf_send.at[order, cs, k, 0])
+
+                    left(slot, hf_send.at[order, cs, k, 1])
 
     for j in range(2):
-        for cs in range(2):
-            left(hbuf.at[j, 2 * x + cs], hf_send.at[j, cs])
-
         @pl.when(x != j)
         def _():
             left(att.at[j], a_send.at[j, 0])
@@ -430,8 +518,8 @@
         scratch_shapes=[
             pltpu.VMEM((2, 4, rows, width), BF16),
             pltpu.VMEM((4, 8, width), F32),
-            pltpu.VMEM((4, 2, width // 2, 3 * head), BF16),
-            pltpu.VMEM((4, width, 2 * head), BF16),
+            pltpu.VMEM((4, 4, width // 4, 3 * head), BF16),
+            pltpu.VMEM((4, 2, width // 2, 2 * head), BF16),
             pltpu.VMEM((2, 8, head), F32),
             pltpu.VMEM((2, 8, head), F32),
             pltpu.VMEM((2, 2 * rows, head), BF16),
@@ -444,8 +532,8 @@
             pltpu.VMEM((8, rows, head), BF16),
             pltpu.VMEM((rows, width), BF16),
             pltpu.VMEM((rows, width), BF16),
-            dma((4,)), dma((2, 4)), dma((2, 2)), dma((4,)), dma((4,)),
-            dma((4,)), dma((4, 2)), dma((4, 3)), dma((4,)), dma((4,)),
+            dma((4, CHUNKS)), dma((2, 4, CHUNKS)), dma((2, 2, CHUNKS, 2)), dma((4,)), dma((4,)),
+            dma((2, 2)), dma((4, 4)), dma((4,)), dma((4, 3)), dma((6,)), dma((4, 2)),
             dma((2,)), dma((2,)), dma((1,)), dma((1,)), dma((1,)), dma((1,)),
             dma((2, 4)), dma((8,)), dma((1,)), dma((1,)),
         ],

time: 86.7 us -> 70.1 us (0.81)
  Pallas kernels: 82.8 us -> 66.2 us
    pallas_call x1, Pallas kernels: 82.8 us -> 66.2 us  [body(): pl.pallas_call(kernel, out_shape=jax.ShapeDtypeStruct((rows, width), BF16...]
where the time goes in v2:
time: 70.1 us; the launch traced here: 70 us
  Pallas kernels  66.2 us (94%)
  local copies, waits for them, and re-layouts  2.3 us (3%)
  between operations  1.42 us (2%)
    pallas_call x1, Pallas kernels, body(): pl.pallas_call(kernel, out_shape=jax.ShapeDtypeStruct((rows, width), BF16...  66.2 us
    unnamed x16, local copies, waits for them, and re-layouts  2.3 us

profile of v2, /device:TPU:1, one launch (start us, length us, event | category | flops | bytes accessed | tf_op | source)
XLA Modules:
  0.0 70.0 jit_solution(16660986579166713307)
XLA Ops:
  1.3 0.0 copy-start
  1.3 0.0 copy-start.1
  1.3 0.0 copy-start.2
  1.3 0.0 copy-start.3
  1.3 0.0 copy-start.4
  1.3 0.0 copy-start.5
  1.4 0.0 copy-start.6
  1.4 1.6 %copy.11 = bf16[96,8,2,384]{3,1,2,0:T(8,128)(2,1)S(1)} copy(bf16[96,8,2,384]{3,2,1,0:T(2,128)(2,1)} %bitcast.3) | data formatting | bytes 2359296
  3.0 0.0 copy-done
  3.0 0.0 copy-done.1
  3.0 0.0 copy-done.2
  3.0 0.0 copy-done.3
  3.0 0.0 copy-done.4
  3.0 0.0 copy-done.5
  3.0 0.0 copy-done.6
  3.0 66.2 %shard_map.100 = bf16[144,768]{1,0:T(8,128)(2,1)S(1)} custom-call(bf16[144,768]{1,0:T(8,128)(2,1)S(1)} %copy-done.2, bf16[3,768]{1,0:T(4,128)(2,1)S(1)} %copy-done.3, bf16[768,768]{1,0:T(8,128)(2,1)S(1)} %bitcast.2, bf16[768,256]{1,0:T(8,128)(2,1)S(1)} %copy-done.1, f32[2,2,128]{2,1,0:T(2,128)S(1)} %copy-done.4, bf16[2,576,256]{2,1,0:T(8,128)(2,1)S(1)} %copy-done, ...), custom_call_target="tpu_custom_call" | custom-call | tf_op jit(solution)/shard_map/pallas_call | solution.py:513
  69.3 0.7 copy.15
Async XLA Ops:
  1.3 1.7 %copy-start = (bf16[2,576,256]{2,1,0:T(8,128)(2,1)S(1)}, bf16[2,576,256]{2,1,0:T(8,128)(2,1)}, u32[]{:S(2)}) copy-start(bf16[2,576,256]{2,1,0:T(8,128)(2,1)} %stale.1) | copy-start | bytes 1769476
  1.3 1.7 %copy-start.1 = (bf16[768,256]{1,0:T(8,128)(2,1)S(1)}, bf16[768,256]{1,0:T(8,128)(2,1)}, u32[]{:S(2)}) copy-start(bf16[768,256]{1,0:T(8,128)(2,1)} %w_out.1) | copy-start | bytes 1179652
  1.3 1.7 %copy-start.2 = (bf16[144,768]{1,0:T(8,128)(2,1)S(1)}, bf16[144,768]{1,0:T(8,128)(2,1)}, u32[]{:S(2)}) copy-start(bf16[144,768]{1,0:T(8,128)(2,1)} %hidden.1) | copy-start | bytes 663556
  1.3 1.7 %copy-start.3 = (bf16[3,768]{1,0:T(4,128)(2,1)S(1)}, bf16[3,768]{1,0:T(4,128)(2,1)}, u32[]{:S(2)}) copy-start(bf16[3,768]{1,0:T(4,128)(2,1)} %mods.1) | copy-start | bytes 13828
  1.3 1.7 %copy-start.4 = (f32[2,2,128]{2,1,0:T(2,128)S(1)}, f32[2,2,128]{2,1,0:T(2,128)}, u32[]{:S(2)}) copy-start(f32[2,2,128]{2,1,0:T(2,128)} %gain.1) | copy-start | bytes 6148
  1.3 1.7 %copy-start.5 = (s32[2,1,2]{2,1,0:T(1,128)S(1)}, s32[2,1,2]{2,1,0:T(1,128)}, u32[]{:S(2)}) copy-start(s32[2,1,2]{2,1,0:T(1,128)} %exponents.1) | copy-start | bytes 52
  1.4 1.7 %copy-start.6 = (f32[1,128]{1,0:T(1,128)S(1)}, f32[1,128]{1,0:T(1,128)}, u32[]{:S(2)}) copy-start(f32[1,128]{1,0:T(1,128)} %constant.2.clone.freqs) | copy-start | bytes 1540

commit v3 on v2

--- a/solution.py
+++ b/solution.py
@@ -13,6 +13,7 @@
 BF16 = jnp.bfloat16
 MESH = pl.DeviceIdType.MESH
 CHUNKS = 3
+BANDS = 1
 
 
 def rotate(values, cosine, sine):
@@ -119,6 +120,7 @@
     rows, width = hidden.shape
     quarter = width // 4
     chunk = rows // CHUNKS
+    band = rows // BANDS
     head = stale.shape[2] // 2
     mine = 2 * rows
     leading = c == lead
@@ -160,25 +162,6 @@
 
     def part_of(j, ts, k):
         return hbuf.at[j, ts, pl.ds(k * chunk, chunk)]
-
-    for k in range(CHUNKS):
-        piece = hidden.at[pl.ds(k * chunk, chunk)]
-        place = part_of(j_mine, t, k)
-        got = h_recv.at[j_mine, t, k]
-
-        @pl.when(z < 3)
-        def _():
-            remote(piece, place, h_send.at[0, k], got, (g, z + 1, 2 * x + target)).start()
-
-        @pl.when(z > 0)
-        def _():
-            remote(piece, place, h_send.at[1, k], got, (g, z - 1, 2 * x + target)).start()
-
-        remote(piece, place, h_send.at[2, k], got, (g, z, 2 * (1 - x) + target)).start()
-
-        @pl.when(c != target)
-        def _():
-            remote(piece, place, h_send.at[3, k], got, sibling).start()
 
     for hl in range(2):
         zt = 2 * c + hl
@@ -195,6 +178,25 @@
                 ).start()
             remote(metasrc.at[hl], meta.at[j_mine], me_send.at[hl], me_recv.at[j_mine],
                    (g, zt, 2 * x + target)).start()
+
+    for k in range(CHUNKS):
+        piece = hidden.at[pl.ds(k * chunk, chunk)]
+        place = part_of(j_mine, t, k)
+        got = h_recv.at[j_mine, t, k]
+
+        @pl.when(z < 3)
+        def _():
+            remote(piece, place, h_send.at[0, k], got, (g, z + 1, 2 * x + target)).start()
+
+        @pl.when(z > 0)
+        def _():
+            remote(piece, place, h_send.at[1, k], got, (g, z - 1, 2 * x + target)).start()
+
+        remote(piece, place, h_send.at[2, k], got, (g, z, 2 * (1 - x) + target)).start()
+
+        @pl.when(c != target)
+        def _():
+            remote(piece, place, h_send.at[3, k], got, sibling).start()
 
     for d in range(1, 4):
         remote(modbuf.at[t], modbuf.at[t], m_send.at[d], m_recv.at[t], (g, z, (t + d) % 4)).start()
@@ -281,32 +283,27 @@
         arrived(slot, got)
         remote(slot, slot, wf_send.at[d, 2], got, sibling).start()
 
-    pass_hidden(0)
-    pass_weight(1)
-    pass_weight(3)
-    pass_hidden(1)
-    pass_weight(2)
-    send_out()
-    for d in (1, 3, 2):
-        pass_weight_far(d)
-
-    place = lax.broadcasted_iota(jnp.int32, (rows, head), 0)
-    lane = lax.broadcasted_iota(jnp.int32, (rows, head), 1)
-    for j in range(2):
-        @pl.when(jnp.logical_not(jnp.logical_and(leading, z % 2 == j)))
-        def _():
-            arrived(meta.at[j], me_recv.at[j])
-
-        positions = jnp.where(place < TXT_DEV, 0.0, meta[j, 4:5, :] + (place - TXT_DEV).astype(F32))
-        angle = positions * freqs[...]
-        cosbuf[pl.ds(j * rows, rows), :] = jnp.cos(angle)
-        sine = jnp.sin(angle)
-        sinbuf[pl.ds(j * rows, rows), :] = jnp.where(lane < head // 2, -sine, sine)
-
-    for d in range(1, 4):
-        arrived(modbuf.at[(t + d) % 4], m_recv.at[(t + d) % 4])
+    def rotary():
+        place = lax.broadcasted_iota(jnp.int32, (rows, head), 0)
+        lane = lax.broadcasted_iota(jnp.int32, (rows, head), 1)
+        for j in range(2):
+            @pl.when(jnp.logical_not(jnp.logical_and(leading, z % 2 == j)))
+            def _():
+                arrived(meta.at[j], me_recv.at[j])
+
+            positions = jnp.where(place < TXT_DEV, 0.0, meta[j, 4:5, :] + (place - TXT_DEV).astype(F32))
+            angle = positions * freqs[...]
+            cosbuf[pl.ds(j * rows, rows), :] = jnp.cos(angle)
+            sine = jnp.sin(angle)
+            sinbuf[pl.ds(j * rows, rows), :] = jnp.where(lane < head // 2, -sine, sine)
+
+    def shifts():
+        for d in range(1, 4):
+            arrived(modbuf.at[(t + d) % 4], m_recv.at[(t + d) % 4])
+
     features = 4 * width
-    for j in range(2):
+
+    def normalise(j):
         for k in range(CHUNKS):
             for cs in range(2):
                 arrived(part_of(j, 2 * (1 - x) + cs, k), h_recv.at[j, 2 * (1 - x) + cs, k])
@@ -328,6 +325,20 @@
             for k in range(4):
                 value = xs[k] * inverse * (1.0 + modbuf[k, 1:2, :]) + modbuf[k, 0:1, :]
                 normed[to, pl.ds(k * width, width)] = value.astype(BF16)
+
+    pass_hidden(0)
+    pass_weight(1)
+    pass_weight(3)
+    pass_hidden(1)
+    pass_weight(2)
+    rotary()
+    pass_weight_far(1)
+    pass_weight_far(3)
+    shifts()
+    normalise(first_j)
+    pass_weight_far(2)
+    send_out()
+    normalise(1 - first_j)
 
     for zs in range(4):
         for core in range(2):
@@ -390,48 +401,60 @@
         weights = jnp.exp(scores - peak)
         weights = (weights / jnp.sum(weights, axis=-1, keepdims=True)).astype(BF16)
         att[j] = jnp.dot(weights, values, preferred_element_type=F32).astype(BF16)
-        for d in range(1, 4):
-            remote(att.at[j], abuf.at[my_head], a_send.at[j, d], a_recv.at[my_head],
-                   (g, (z + d) % 4, 2 * j + c)).start()
-
-        @pl.when(x == j)
-        def _():
-            abuf[my_head] = att[j]
-
-        @pl.when(x != j)
-        def _():
-            remote(att.at[j], abuf.at[my_head], a_send.at[j, 0], a_recv.at[my_head], (g, z, 2 * j + c)).start()
+
+    for n in range(BANDS):
+        at = pl.ds(n * band, band)
+        for j in range(2):
+            source, place, got = att.at[j, at], abuf.at[my_head, at], a_recv.at[my_head, n]
+            for d in range(1, 4):
+                remote(source, place, a_send.at[j, d, n], got, (g, (z + d) % 4, 2 * j + c)).start()
+
+            @pl.when(x != j)
+            def _():
+                remote(source, place, a_send.at[j, 0, n], got, (g, z, 2 * j + c)).start()
+
+    @pl.when(x == 0)
+    def _():
+        abuf[my_head] = att[0]
+
+    @pl.when(x == 1)
+    def _():
+        abuf[my_head] = att[1]
 
     for part in range(2):
         for ts in (2 * x + 1 - c, 2 * (1 - x) + 1 - c):
             arrived(wobuf.at[ts, part], wo_recv.at[ts, part])
-    for h in range(8):
-        @pl.when(h != my_head)
-        def _():
-            arrived(abuf.at[h], a_recv.at[h])
-
-    total = None
-    for k in range(4):
-        pair = jnp.concatenate([abuf[2 * k], abuf[2 * k + 1]], axis=-1)
-        value = lax.dot_general(pair, wobuf[k].reshape(width, 2 * head), (((1,), (1,)), ((), ())), preferred_element_type=F32)
-        total = value if total is None else total + value
-    res[...] = (hbuf[x, z].astype(F32) + modbuf[z, 2:3, :] * total).astype(BF16)
     owner = 2 * c + x
     home = jnp.logical_and(owner == z, z == t)
-
-    @pl.when(home)
-    def _():
-        landed[...] = res[...]
-
-    @pl.when(jnp.logical_not(home))
-    def _():
-        remote(res, landed, r_send.at[0], r_recv.at[0], (g, owner, z)).start()
+    for n in range(BANDS):
+        at = pl.ds(n * band, band)
+        for h in range(8):
+            @pl.when(h != my_head)
+            def _():
+                arrived(abuf.at[h, at], a_recv.at[h, n])
+
+        total = None
+        for k in range(4):
+            pair = jnp.concatenate([abuf[2 * k, at], abuf[2 * k + 1, at]], axis=-1)
+            value = lax.dot_general(
+                pair, wobuf[k].reshape(width, 2 * head), (((1,), (1,)), ((), ())), preferred_element_type=F32
+            )
+            total = value if total is None else total + value
+        res[at] = (hbuf[x, z, at].astype(F32) + modbuf[z, 2:3, :] * total).astype(BF16)
+
+        @pl.when(home)
+        def _():
+            landed[at] = res[at]
+
+        @pl.when(jnp.logical_not(home))
+        def _():
+            remote(res.at[at], landed.at[at], r_send.at[n], r_recv.at[n], (g, owner, z)).start()
 
     from_self = jnp.logical_and(t == z, 2 * (z % 2) + z // 2 == t)
-
-    @pl.when(jnp.logical_not(from_self))
-    def _():
-        arrived(landed, r_recv.at[0])
+    for n in range(BANDS):
+        @pl.when(jnp.logical_not(from_self))
+        def _():
+            arrived(landed.at[pl.ds(n * band, band)], r_recv.at[n])
 
     out[...] = landed[...]
 
@@ -447,7 +470,8 @@
             left(wbuf.at[(z + d) % 4, 2 * g + c], wf_send.at[d, k])
         left(wbuf.at[(z + d) % 4, 2 * (1 - g) + c], wf_send.at[d, 2])
         for j in range(2):
-            left(att.at[j], a_send.at[j, d])
+            for n in range(BANDS):
+                left(att.at[j, pl.ds(n * band, band)], a_send.at[j, d, n])
     for k in range(6):
         left(wobuf.at[t, 0], wo_send.at[k])
     for k in range(CHUNKS):
@@ -493,12 +517,14 @@
     for j in range(2):
         @pl.when(x != j)
         def _():
-            left(att.at[j], a_send.at[j, 0])
+            for n in range(BANDS):
+                left(att.at[j, pl.ds(n * band, band)], a_send.at[j, 0, n])
     left(kv.at[:, ours, :], kv_send.at[0])
 
     @pl.when(jnp.logical_not(home))
     def _():
-        left(res, r_send.at[0])
+        for n in range(BANDS):
+            left(res.at[pl.ds(n * band, band)], r_send.at[n])
 
 
 def body(hidden, modulation, w_qkv, w_out, qk_gain, stale, offsets, text_count, exponents):
@@ -535,7 +561,7 @@
             dma((4, CHUNKS)), dma((2, 4, CHUNKS)), dma((2, 2, CHUNKS, 2)), dma((4,)), dma((4,)),
             dma((2, 2)), dma((4, 4)), dma((4,)), dma((4, 3)), dma((6,)), dma((4, 2)),
             dma((2,)), dma((2,)), dma((1,)), dma((1,)), dma((1,)), dma((1,)),
-            dma((2, 4)), dma((8,)), dma((1,)), dma((1,)),
+            dma((2, 4, BANDS)), dma((8, BANDS)), dma((BANDS,)), dma((BANDS,)),
         ],
         compiler_params=pltpu.CompilerParams(
             collective_id=0, has_side_effects=True, vmem_limit_bytes=40 * 2**20

time: 70.1 us -> 69.4 us (0.990)
    pallas_call x1, Pallas kernels: 66.2 us -> 65.5 us  [body(): pl.pallas_call(kernel, out_shape=jax.ShapeDtypeStruct((rows, width), BF16...]
where the time goes in v3:
time: 69.4 us; the launch traced here: 69.2 us
  Pallas kernels  65.5 us (94%)
  local copies, waits for them, and re-layouts  2.3 us (3%)
  between operations  1.42 us (2%)
    pallas_call x1, Pallas kernels, body(): pl.pallas_call(kernel, out_shape=jax.ShapeDtypeStruct((rows, width), BF16...  65.5 us
    unnamed x16, local copies, waits for them, and re-layouts  2.3 us

profile of v3, /device:TPU:1, one launch (start us, length us, event | category | flops | bytes accessed | tf_op | source)
XLA Modules:
  0.0 69.2 jit_solution(1703643759156889240)
XLA Ops:
  1.3 0.0 copy-start
  1.3 0.0 copy-start.1
  1.3 0.0 copy-start.2
  1.3 0.0 copy-start.3
  1.3 0.0 copy-start.4
  1.3 0.0 copy-start.5
  1.4 0.0 copy-start.6
  1.4 1.6 %copy.11 = bf16[96,8,2,384]{3,1,2,0:T(8,128)(2,1)S(1)} copy(bf16[96,8,2,384]{3,2,1,0:T(2,128)(2,1)} %bitcast.3) | data formatting | bytes 2359296
  3.0 0.0 copy-done
  3.0 0.0 copy-done.1
  3.0 0.0 copy-done.2
  3.0 0.0 copy-done.3
  3.0 0.0 copy-done.4
  3.0 0.0 copy-done.5
  3.0 0.0 copy-done.6
  3.0 65.5 %shard_map.100 = bf16[144,768]{1,0:T(8,128)(2,1)S(1)} custom-call(bf16[144,768]{1,0:T(8,128)(2,1)S(1)} %copy-done.2, bf16[3,768]{1,0:T(4,128)(2,1)S(1)} %copy-done.3, bf16[768,768]{1,0:T(8,128)(2,1)S(1)} %bitcast.2, bf16[768,256]{1,0:T(8,128)(2,1)S(1)} %copy-done.1, f32[2,2,128]{2,1,0:T(2,128)S(1)} %copy-done.4, bf16[2,576,256]{2,1,0:T(8,128)(2,1)S(1)} %copy-done, ...), custom_call_target="tpu_custom_call" | custom-call | tf_op jit(solution)/shard_map/pallas_call | solution.py:539
  68.5 0.7 copy.15
Async XLA Ops:
  1.3 1.7 %copy-start = (bf16[2,576,256]{2,1,0:T(8,128)(2,1)S(1)}, bf16[2,576,256]{2,1,0:T(8,128)(2,1)}, u32[]{:S(2)}) copy-start(bf16[2,576,256]{2,1,0:T(8,128)(2,1)} %stale.1) | copy-start | bytes 1769476
  1.3 1.7 %copy-start.1 = (bf16[768,256]{1,0:T(8,128)(2,1)S(1)}, bf16[768,256]{1,0:T(8,128)(2,1)}, u32[]{:S(2)}) copy-start(bf16[768,256]{1,0:T(8,128)(2,1)} %w_out.1) | copy-start | bytes 1179652
  1.3 1.7 %copy-start.2 = (bf16[144,768]{1,0:T(8,128)(2,1)S(1)}, bf16[144,768]{1,0:T(8,128)(2,1)}, u32[]{:S(2)}) copy-start(bf16[144,768]{1,0:T(8,128)(2,1)} %hidden.1) | copy-start | bytes 663556
  1.3 1.7 %copy-start.3 = (bf16[3,768]{1,0:T(4,128)(2,1)S(1)}, bf16[3,768]{1,0:T(4,128)(2,1)}, u32[]{:S(2)}) copy-start(bf16[3,768]{1,0:T(4,128)(2,1)} %mods.1) | copy-start | bytes 13828
  1.3 1.7 %copy-start.4 = (f32[2,2,128]{2,1,0:T(2,128)S(1)}, f32[2,2,128]{2,1,0:T(2,128)}, u32[]{:S(2)}) copy-start(f32[2,2,128]{2,1,0:T(2,128)} %gain.1) | copy-start | bytes 6148
  1.3 1.7 %copy-start.5 = (s32[2,1,2]{2,1,0:T(1,128)S(1)}, s32[2,1,2]{2,1,0:T(1,128)}, u32[]{:S(2)}) copy-start(s32[2,1,2]{2,1,0:T(1,128)} %exponents.1) | copy-start | bytes 52
  1.4 1.7 %copy-start.6 = (f32[1,128]{1,0:T(1,128)S(1)}, f32[1,128]{1,0:T(1,128)}, u32[]{:S(2)}) copy-start(f32[1,128]{1,0:T(1,128)} %constant.2.clone.freqs) | copy-start | bytes 1540
